TPU v7x, 512 devices: a whole 4x4x16 slice. The times are simulated.
512 devices in a mesh: tri: 64 (over y, z), sub: 8 (over x, core).
Axes of the slice: x: 4, y: 4, z: 16, core: 2. Of those that a mesh axis runs over, the one named last changes fastest.
Arguments:
- stored_tiles: float32 [64, 10, 512, 512], P('tri', None, 'sub'), may hold values from -190 to 190, as said below
- cell_owner: int32 [64], replicated, may hold values from 0 to 63, as said below
Outputs:
- updated: float32 [64, 10, 512, 512], P('tri', None, 'sub')
Inputs may be any that keep to these rules, and one draw needn't show every extreme that they name: `cell_owner`: a permutation of the indices of tri. `stored_tiles`: every tile whose row and column blocks are equal is skew-symmetric, every pivot met is invertible, and slots that hold no tile are zero.
All inputs are finite; a program needn't handle non-finite values.
Results may differ from a plain program's by a relative error of at most 0.00035.
Values may be sent and summed in bfloat16 or wider, within the bound.
A program may use at most 64 MiB of HBM per device.

v0:
```python
import math
import jax
import jax.numpy as jnp
import numpy as np
from jax import lax
from jax.sharding import Mesh
from jax.sharding import PartitionSpec as P

NB = 32
TRI = ("tri_0", "tri_1")


def in_order(tiles, dim):
    tiles = jnp.moveaxis(tiles, 0, dim)
    dims = tiles.shape
    return tiles.reshape(*dims[:dim], dims[dim] * dims[dim + 1], *dims[dim + 2 :])


def gather_in_order(x, axes, turns):
    tiles = x[None]
    for k in turns:
        tiles = lax.all_gather(tiles, axes[k], axis=0, tiled=True)
    block = [lax.axis_size(axes[k]) for k in reversed(turns)]
    tiles = tiles.reshape(*block, *x.shape)
    turned = sorted(range(len(turns)), key=lambda place: turns[len(turns) - 1 - place])
    return tiles.transpose(*turned, *range(len(turns), tiles.ndim)).reshape(-1, *x.shape)


def gather_axes(x, axes, turns, dim):
    return in_order(gather_in_order(x, axes, turns), dim)


def layout(groups, per_group):
    half_group = per_group // 2
    slot_count = per_group * (per_group + 1) // 2
    row_table = np.full((groups * groups, slot_count), -1, np.int32)
    col_table = np.full((groups * groups, slot_count), -1, np.int32)
    for first_group in range(groups):
        for second_group in range(groups):
            cell_index = first_group * groups + second_group
            for inner_row in range(per_group):
                if first_group == second_group:
                    for inner_column in range(inner_row + 1):
                        slot_index = inner_row * (inner_row + 1) // 2 + inner_column
                        row_table[cell_index, slot_index] = first_group * per_group + inner_row
                        col_table[cell_index, slot_index] = first_group * per_group + inner_column
                else:
                    for inner_column in range(half_group):
                        slot_index = inner_row * half_group + inner_column
                        if first_group > second_group:
                            row_table[cell_index, slot_index] = first_group * per_group + inner_row
                            col_table[cell_index, slot_index] = (
                                second_group * per_group + inner_column
                            )
                        else:
                            row_table[cell_index, slot_index] = second_group * per_group + inner_row
                            col_table[cell_index, slot_index] = (
                                first_group * per_group + half_group + inner_column
                            )
    return (row_table, col_table)


def shards(stored_tiles, cell_owner):
    tri_count = lax.axis_size(TRI)
    groups = math.isqrt(tri_count)
    per_group = NB // groups
    half_group = per_group // 2
    strip_rows = stored_tiles.shape[2]
    block_order = stored_tiles.shape[3]
    row_table, col_table = layout(groups, per_group)
    position = lax.axis_index(TRI)
    my_cell = jnp.sum(jnp.where(cell_owner == position, jnp.arange(tri_count, dtype=jnp.int32), 0))
    cell_down = my_cell // groups
    cell_across = my_cell % groups
    row_group = jnp.maximum(cell_down, cell_across)
    col_group = jnp.minimum(cell_down, cell_across)
    my_rows = jnp.asarray(row_table)[my_cell]
    my_cols = jnp.asarray(col_table)[my_cell]
    row_local = jnp.clip(my_rows - row_group * per_group, 0, per_group - 1)
    col_local = jnp.clip(my_cols - col_group * per_group, 0, per_group - 1)
    holders = cell_owner[jnp.arange(groups) * groups]
    highest = lax.Precision.HIGHEST
    current = stored_tiles[0]
    lower_slots = np.array([member * half_group for member in range(per_group)], np.int32)
    first_slots = np.array(
        [member * (member + 1) // 2 if member > 0 else 0 for member in range(per_group)], np.int32
    )
    keep_first = np.array([1.0 if member > 0 else 0.0 for member in range(per_group)], np.float32)
    from_lower = current[lower_slots]
    from_first = current[first_slots] * keep_first[:, None, None]
    holder_part = jnp.where(cell_down > 0, from_lower, from_first)
    holder_part = jnp.where(cell_across == 0, holder_part, 0.0).astype(jnp.bfloat16)
    pivot_slot = 0 // 2
    pivot_part = jnp.where(my_cell == 0, current[pivot_slot], 0.0)
    piece_size = holder_part.size // tri_count
    spread_panel = lax.all_to_all(
        holder_part.reshape(tri_count, piece_size), TRI, split_axis=0, concat_axis=0, tiled=True
    )
    spread_pivot = lax.all_to_all(
        pivot_part.astype(jnp.bfloat16), TRI, split_axis=0, concat_axis=0, tiled=True
    ).astype(pivot_part.dtype)
    picked_panel = spread_panel[holders][:, None, :]
    picked_pivot = spread_pivot[holders[0]][None, :]
    whole_panel = gather_axes(picked_panel, TRI, (0, 1), 1)
    whole_pivot = gather_axes(picked_pivot.astype(jnp.bfloat16), TRI, (0, 1), 0).astype(
        picked_pivot.dtype
    )
    panels = whole_panel.reshape(groups, per_group, strip_rows, block_order)
    own_strips = panels[row_group]
    other_strips = panels[col_group]
    pivot_block = lax.all_gather(
        whole_pivot.astype(jnp.bfloat16), "sub", axis=0, tiled=True
    ).astype(whole_pivot.dtype)
    partner = lax.all_gather(other_strips, "sub", axis=1, tiled=True)
    gram_matrix = jnp.dot(pivot_block.T, pivot_block, precision=highest)
    factor = jnp.linalg.cholesky(gram_matrix)
    inverse = jax.scipy.linalg.cho_solve((factor, True), pivot_block.T)
    scaled = jnp.einsum(
        "irk,kc->irc", own_strips.astype(jnp.float32), inverse, precision=highest
    ).astype(jnp.bfloat16)
    left_slots = scaled[row_local]
    right_slots = partner[col_local]
    update = jnp.einsum("qrk,qck->qrc", left_slots, right_slots, preferred_element_type=jnp.float32)
    live_slots = (my_rows > 0) & (my_cols > 0)
    current = current + jnp.where(live_slots[:, None, None], update, 0.0)
    return current[None]


def solution(mesh):
    torus = Mesh(mesh.devices.reshape(4, 16, mesh.shape["sub"]), ("tri_0", "tri_1", "sub"))
    return jax.shard_map(
        shards,
        mesh=torus,
        in_specs=(P(TRI, None, "sub", None), P()),
        out_specs=P(TRI, None, "sub", None),
        check_vma=False,
    )
```

profile of v0, /device:TPU:1, one launch (start us, length us, event | category | flops | bytes accessed | tf_op | source)
XLA Modules:
  0.0 323.7 jit_solution(5538113034983923474)
XLA Ops:
  6.5 1.4 fusion.56
  8.6 0.9 fusion.39
  9.5 0.5 broadcast.463
  10.0 0.6 reduce.25
  10.6 0.6 reshape.305
  11.3 19.3 %all-to-all-start.1 = ((bf16[64,2,256]{2,1,0:T(2,128)(2,1)}), bf16[64,2,256]{2,1,0:T(2,128)(2,1)S(1)}, u32[]{:S(2)}, u32[]{:S(2)}) async-start(bf16[64,2,256]{2,1,0:T(2,128)(2,1)} %reshape.305), calls=%async_computation.1 | async-start | bytes 131072 | tf_op jit(solution)/shard_map/all_to_all | solution.py:99
  33.4 1.3 gather_fusion.2
  34.7 0.7 pad_clamp_fusion.4
  35.4 1.9 gather_fusion.1
  37.3 1.9 gather_fusion
  40.6 0.7 fusion.59
  41.3 0.7 and_bitcast_fusion
  42.2 0.7 fusion.60
  43.2 2.1 reduce.26
  45.2 0.9 reshape.307
  46.2 14.6 %all-to-all-start = ((bf16[64,2,1024]{2,1,0:T(2,128)(2,1)}), bf16[64,2,1024]{2,1,0:T(2,128)(2,1)S(1)}, u32[]{:S(2)}, u32[]{:S(2)}) async-start(bf16[64,2,1024]{2,1,0:T(2,128)(2,1)} %reshape.307), calls=%async_computation | async-start | bytes 524288 | tf_op jit(solution)/shard_map/all_to_all | solution.py:96
  60.9 8.8 %all_gather.20 = bf16[4,1,512]{2,1,0:T(2,128)(2,1)S(1)} all-gather(bf16[1,1,512]{2,1,0:T(2,128)(2,1)S(1)} %fusion.54), channel_id=1, replica_groups=mesh['tri_0'=4,'tri_1'=16,'sub'=8] {'tri_0'}, dimensions={0}, use_global_device_ids=true | all-gather | bytes 5120 | tf_op jit(solution)/shard_map/all_gather | solution.py:22
  69.7 23.8 %all_gather.21 = bf16[64,1,512]{2,1,0:T(2,128)(2,1)S(1)} all-gather(bf16[4,1,512]{2,1,0:T(2,128)(2,1)S(1)} %all_gather.20), channel_id=1, replica_groups=mesh['tri_0'=4,'tri_1'=16,'sub'=8] {'tri_1'}, dimensions={0}, use_global_device_ids=true | all-gather | bytes 69632 | tf_op jit(solution)/shard_map/all_gather | solution.py:22
  93.9 23.9 %all_gather.22 = bf16[512,512]{1,0:T(8,128)(2,1)S(1)} all-gather(bf16[64,512]{1,0:T(8,128)(2,1)S(1)} %bitcast.120), channel_id=1, replica_groups=mesh['tri_0'=4,'tri_1'=16,'sub'=8] {'sub'}, dimensions={0}, use_global_device_ids=true | all-gather | bytes 589824 | tf_op jit(solution)/shard_map/all_gather | solution.py:111
  117.8 0.5 fusion.67
  118.9 1.0 copy-done.1
  119.9 11.7 %cholesky.104 = f32[128,128]{1,0:T(8,128)S(1)} custom-call(f32[128,128]{1,0:T(8,128)S(1)} %cholesky.266), custom_call_target="Cholesky" | custom-call | tf_op jit(solution)/shard_map/jit(cholesky)/cholesky | solution.py:116
  131.6 9.8 %custom-call.34 = f32[1,128,128]{1,2,0:T(8,128)S(1)} custom-call(f32[1,128,128]{2,1,0:T(8,128)S(1)} %get-tuple-element.32), custom_call_target="InvertDiagBlocksLowerTriangular" | custom-call | tf_op jit(solution)/shard_map/jit(cholesky)/cholesky | solution.py:116
  142.0 0.6 gather_fusion.3
  142.6 9.8 %all-gather = bf16[32,2048]{1,0:T(8,128)(2,1)} all-gather(bf16[8,2048]{1,0:T(8,128)(2,1)S(1)} %gather_fusion.3), channel_id=2, replica_groups=mesh['tri_0'=4,'tri_1'=16,'sub'=8] {'tri_0'}, dimensions={0}, use_global_device_ids=true | all-gather | bytes 163840 | tf_op jit(solution)/shard_map/all_gather | solution.py:22
  153.0 1.0 copy.32
  154.3 11.7 %cholesky.217 = f32[128,128]{1,0:T(8,128)S(1)} custom-call(f32[128,128]{1,0:T(8,128)S(1)} %cholesky.270), custom_call_target="Cholesky" | custom-call | tf_op jit(solution)/shard_map/jit(cholesky)/cholesky | solution.py:116
  166.1 9.8 %custom-call.35 = f32[1,128,128]{1,2,0:T(8,128)S(1)} custom-call(f32[1,128,128]{2,1,0:T(8,128)S(1)} %get-tuple-element.29), custom_call_target="InvertDiagBlocksLowerTriangular" | custom-call | tf_op jit(solution)/shard_map/jit(cholesky)/cholesky | solution.py:116
  176.6 11.7 %cholesky.238 = f32[128,128]{1,0:T(8,128)S(1)} custom-call(f32[128,128]{1,0:T(8,128)S(1)} %cholesky.275), custom_call_target="Cholesky" | custom-call | tf_op jit(solution)/shard_map/jit(cholesky)/cholesky | solution.py:116
  188.3 10.0 %custom-call.36 = f32[1,128,128]{1,2,0:T(8,128)S(1)} custom-call(f32[1,128,128]{2,1,0:T(8,128)S(1)} %get-tuple-element.26), custom_call_target="InvertDiagBlocksLowerTriangular" | custom-call | tf_op jit(solution)/shard_map/jit(cholesky)/cholesky | solution.py:116
  198.5 0.4 convolution_subtract_fusion.8
  198.9 11.7 %cholesky.255 = f32[128,128]{1,0:T(8,128)S(1)} custom-call(f32[128,128]{1,0:T(8,128)S(1)} %convolution_subtract_fusion.8), custom_call_target="Cholesky" | custom-call | tf_op jit(solution)/shard_map/jit(cholesky)/cholesky | solution.py:116
  210.6 0.7 compare_reduce_fusion.2
  212.7 0.7 compare_reduce_fusion.1
  214.1 0.7 compare_reduce_fusion
  215.7 10.8 %while.1 = (s32[]{:T(128)}, f32[512,512]{1,0:T(8,128)S(1)}, s32[4,2]{0,1:T(2,128)S(1)}, f32[4,128,128]{2,1,0:T(8,128)}, s32[]{:T(128)}) while((s32[]{:T(128)}, f32[512,512]{1,0:T(8,128)S(1)}, s32[4,2]{0,1:T(2,128)S(1)}, f32[4,128,128]{2,1,0:T(8,128)}, s32[]{:T(128)}) %tuple.27), condition=%wide.while_cond, body=%wide.while_body.sunk | while | flops 2 | bytes 132705 | solution.py:117
  215.8 0.6 fusion.83
  216.4 2.0 bitcast_dynamic-update-slice_fusion.2
  218.5 0.6 fusion.83
  219.1 2.0 bitcast_dynamic-update-slice_fusion.2
  221.2 0.6 fusion.83
  221.8 2.0 bitcast_dynamic-update-slice_fusion.2
  223.9 0.6 fusion.83
  224.5 2.0 bitcast_dynamic-update-slice_fusion.2
  226.5 40.1 %custom-call.37 = f32[4,128,128]{1,2,0:T(8,128)S(1)} custom-call(f32[4,128,128]{2,1,0:T(8,128)} %get-tuple-element.12), custom_call_target="InvertDiagBlocksLowerTriangular" | custom-call | tf_op jit(solution)/shard_map/jit(_cho_solve)/triangular_solve | solution.py:117
  266.7 1.7 copy.27
  268.4 1.2 copy.28
  269.6 2.6 reshape_reshape.6
  272.2 1.7 constant_dynamic-slice_fusion.1
  273.9 1.2 fusion.35
  275.1 1.2 bitcast_convert_fusion
  276.7 0.4 fusion.49
  277.1 0.4 convolution_subtract_fusion.2
  277.5 0.4 fusion.51
  278.0 0.6 convolution_subtract_fusion.5
  278.6 0.4 fusion.53
  279.4 0.4 convolution_subtract_fusion.1
  280.2 0.5 convolution_subtract_fusion
  281.0 0.7 convolution_subtract_fusion.4
  282.1 1.6 convolution_convert_fusion
  283.7 0.6 gather_fusion.4
  284.3 21.5 %all-gather.7.cloned.1.call-done = bf16[1,4,512,512]{3,2,1,0:T(8,128)(2,1)} async-done(((bf16[1,4,64,512]{3,2,1,0:T(8,128)(2,1)}), bf16[1,4,512,512]{3,2,1,0:T(8,128)(2,1)}) %all-gather.7.cloned.1.call-update) | async-done | bytes 2097168 | tf_op jit(solution)/shard_map/all_gather | solution.py:114
  305.8 5.5 %gather_fusion.5 = bf16[10,512,512]{2,1,0:T(8,128)(2,1)} fusion(bf16[4,512,512]{2,1,0:T(8,128)(2,1)} %bitcast.112, s32[1024]{0:T(1024)S(1)} %pad_clamp_fusion), kind=kCustom, calls=%fused_computation.5 | custom fusion | bytes 10485800 | tf_op jit(solution)/shard_map/gather | solution.py:122
  311.4 5.2 %fusion.1 = f32[1,10,64,512]{3,2,1,0:T(8,128)} fusion(bf16[10,64,512]{2,1,0:T(8,128)(2,1)S(1)} %gather_fusion.4, bf16[10,512,512]{2,1,0:T(8,128)(2,1)} %gather_fusion.5, pred[10]{0:T(512)(128)(4,1)S(1)} %and_bitcast_fusion, f32[1,10,64,512]{3,2,1,0:T(8,128)S(1)} %copy-done), kind=kOutput, calls=%fused_computation.10 | convolution fusion | flops 336199680 | bytes 8519690 | tf_op jit(solution)/shard_map/qrk,qck->qrc/dot_general | solution.py:123
  (59 shorter events, 6.1 us)
Async XLA Ops:
  6.5 35.5 %copy-start.3 = (f32[4]{0:T(128)S(1)}, f32[4]{0:T(128)}, u32[]{:S(2)}) copy-start(f32[4]{0:T(128)} %constant.245) | copy-start | bytes 52
  11.3 34.9 %all-to-all-start.1 = ((bf16[64,2,256]{2,1,0:T(2,128)(2,1)}), bf16[64,2,256]{2,1,0:T(2,128)(2,1)S(1)}, u32[]{:S(2)}, u32[]{:S(2)}) async-start(bf16[64,2,256]{2,1,0:T(2,128)(2,1)} %reshape.305), calls=%async_computation.1 | async-start | bytes 131072 | tf_op jit(solution)/shard_map/all_to_all | solution.py:99
  46.2 95.4 %all-to-all-start = ((bf16[64,2,1024]{2,1,0:T(2,128)(2,1)}), bf16[64,2,1024]{2,1,0:T(2,128)(2,1)S(1)}, u32[]{:S(2)}, u32[]{:S(2)}) async-start(bf16[64,2,1024]{2,1,0:T(2,128)(2,1)} %reshape.307), calls=%async_computation | async-start | bytes 524288 | tf_op jit(solution)/shard_map/all_to_all | solution.py:96
  60.8 205.9 %all-gather.5.cloned.1.call-start = ((), (), s32[]{:S(2)}) async-start(), calls=%async_computation.2 | async-start | bytes 2228224 | tf_op jit(solution)/shard_map/all_gather | solution.py:22
  118.9 1.0 copy-start.1
  119.9 32.8 %copy-start.2 = (f32[512,512]{1,0:T(8,128)S(1)}, f32[512,512]{1,0:T(8,128)}, u32[]{:S(2)}) copy-start(f32[512,512]{1,0:T(8,128)} %copy-done.1) | copy-start | bytes 3145732
  152.4 153.4 %all-gather.7.cloned.1.call-start = ((), (), s32[]{:S(2)}) async-start(), calls=%async_computation.3 | async-start | bytes 2359296 | tf_op jit(solution)/shard_map/all_gather | solution.py:114
  305.8 5.6 %copy-start = (f32[1,10,64,512]{3,2,1,0:T(8,128)S(1)}, f32[1,10,64,512]{3,2,1,0:T(8,128)}, u32[]{:S(2)}) copy-start(f32[1,10,64,512]{3,2,1,0:T(8,128)} %param.9) | copy-start | bytes 3932164
Sparse Core Ops, SparseCore 0:
  152.6 63.2 all-gather.4
  274.0 31.7 all-gather.6
where the time goes:
time: 329 us; the launch traced here: 324 us
  other arithmetic  129 us (39%)
  blocking collectives  66.3 us (20%)
  local copies, waits for them, and re-layouts  34.9 us (11%)
  starting transfers between devices  34.1 us (10%)
  between operations  21.9 us (7%)
  waiting for transfers between devices  21.6 us (7%)
  matrix products  16.1 us (5%)
    another operation x14, other arithmetic, shards(): factor = jnp.linalg.cholesky(gram_matrix)  78.8 us
    all_gather x3, blocking collectives, gather_in_order(): tiles = lax.all_gather(tiles, axes[k], axis=0, tiled=True)  42.5 us
    another operation x3, other arithmetic, shards(): inverse = jax.scipy.linalg.cho_solve((factor, True), pivot_block.T)  40.3 us
    all_gather x1, blocking collectives, shards(): lax.all_gather(whole_pivot.astype(jnp.bfloat16), 'sub', axis=0, tiled=True)  23.9 us
    all_gather x1, waiting for transfers between devices, shards(): partner = lax.all_gather(other_strips, 'sub', axis=1, tiled=True)  21.5 us
    all_to_all x1, starting transfers between devices, shards(): lax.all_to_all(pivot_part.astype(jnp.bfloat16), TRI, split_axis=0, concat...  19.3 us
    all_to_all x1, starting transfers between devices, shards(): lax.all_to_all(holder_part.reshape(tri_count, piece_size), TRI, split_axi...  14.6 us
    another operation x12, local copies, waits for them, and re-layouts  10.8 us
  transfers between devices with their start and end apart: 4, of which 1 were waited for; matrix products, arithmetic and copies ran while one was open for 48% of the time, Pallas kernels for 0%

commit v1 on v0

--- a/solution.py
+++ b/solution.py
@@ -111,7 +111,9 @@
     pivot_block = lax.all_gather(
         whole_pivot.astype(jnp.bfloat16), "sub", axis=0, tiled=True
     ).astype(whole_pivot.dtype)
-    partner = lax.all_gather(other_strips, "sub", axis=1, tiled=True)
+    partner = jnp.concatenate(
+        lax.all_to_all(jnp.stack([other_strips] * lax.axis_size("sub")), "sub", 0, 0), axis=1
+    )
     gram_matrix = jnp.dot(pivot_block.T, pivot_block, precision=highest)
     factor = jnp.linalg.cholesky(gram_matrix)
     inverse = jax.scipy.linalg.cho_solve((factor, True), pivot_block.T)

time: 329 us -> 340 us (1.033)
  starting transfers between devices: 34.1 us -> 41.6 us
  matrix products: 16.1 us -> 19.7 us
    all_gather x1 -> x0, waiting for transfers between devices: 21.5 us -> none  [shards(): partner = lax.all_gather(other_strips, 'sub', axis=1, tiled=True)]
    all_to_all x0 -> x1, waiting for transfers between devices: none -> 19.7 us  [shards(): lax.all_to_all(jnp.stack([other_strips] * lax.axis_size('sub')), 'sub', 0...]
    all_to_all x0 -> x1, starting transfers between devices: none -> 7.7 us  [shards(): lax.all_to_all(jnp.stack([other_strips] * lax.axis_size('sub')), 'sub', 0...]
    another operation x6, matrix products: 1.86 us -> 5.46 us  [shards(): factor = jnp.linalg.cholesky(gram_matrix)]
    another operation x12 -> x13, local copies, waits for them, and re-layouts: 10.8 us -> 12.4 us
where the time goes in v1:
time: 340 us; the launch traced here: 335 us
  other arithmetic  128 us (38%)
  blocking collectives  66.6 us (20%)
  starting transfers between devices  41.6 us (12%)
  local copies, waits for them, and re-layouts  36.5 us (11%)
  between operations  21.9 us (6%)
  waiting for transfers between devices  19.8 us (6%)
  matrix products  19.7 us (6%)
    another operation x14, other arithmetic, shards(): factor = jnp.linalg.cholesky(gram_matrix)  78.6 us
    all_gather x3, blocking collectives, gather_in_order(): tiles = lax.all_gather(tiles, axes[k], axis=0, tiled=True)  42.7 us
    another operation x3, other arithmetic, shards(): inverse = jax.scipy.linalg.cho_solve((factor, True), pivot_block.T)  40.3 us
    all_gather x1, blocking collectives, shards(): lax.all_gather(whole_pivot.astype(jnp.bfloat16), 'sub', axis=0, tiled=True)  24 us
    all_to_all x1, waiting for transfers between devices, shards(): lax.all_to_all(jnp.stack([other_strips] * lax.axis_size('sub')), 'sub', 0...  19.7 us
    all_to_all x1, starting transfers between devices, shards(): lax.all_to_all(pivot_part.astype(jnp.bfloat16), TRI, split_axis=0, concat...  19.3 us
    all_to_all x1, starting transfers between devices, shards(): lax.all_to_all(holder_part.reshape(tri_count, piece_size), TRI, split_axi...  14.6 us
    another operation x12, local copies, waits for them, and re-layouts  10.9 us
  transfers between devices with their start and end apart: 4, of which 1 were waited for; matrix products, arithmetic and copies ran while one was open for 48% of the time, Pallas kernels for 0%

profile of v1, /device:TPU:1, one launch (start us, length us, event | category | flops | bytes accessed | tf_op | source)
XLA Modules:
  0.0 334.6 jit_solution(18107565832825047004)
XLA Ops:
  6.5 1.4 fusion.56
  8.6 0.9 fusion.39
  9.5 0.5 broadcast.464
  10.0 0.6 reduce.25
  10.6 0.6 reshape.313
  11.3 19.3 %all-to-all-start.1 = ((bf16[64,2,256]{2,1,0:T(2,128)(2,1)}), bf16[64,2,256]{2,1,0:T(2,128)(2,1)S(1)}, u32[]{:S(2)}, u32[]{:S(2)}) async-start(bf16[64,2,256]{2,1,0:T(2,128)(2,1)} %reshape.313), calls=%async_computation.1 | async-start | bytes 131072 | tf_op jit(solution)/shard_map/all_to_all | solution.py:99
  34.8 0.7 fusion.59
  35.5 0.7 and_bitcast_fusion
  36.2 1.3 gather_fusion.2
  37.5 0.7 pad_clamp_fusion.4
  38.2 1.9 gather_fusion
  40.1 1.9 gather_fusion.1
  42.2 0.7 fusion.60
  43.1 2.1 reduce.26
  45.2 0.9 reshape.315
  46.2 14.6 %all-to-all-start = ((bf16[64,2,1024]{2,1,0:T(2,128)(2,1)}), bf16[64,2,1024]{2,1,0:T(2,128)(2,1)S(1)}, u32[]{:S(2)}, u32[]{:S(2)}) async-start(bf16[64,2,1024]{2,1,0:T(2,128)(2,1)} %reshape.315), calls=%async_computation | async-start | bytes 524288 | tf_op jit(solution)/shard_map/all_to_all | solution.py:96
  60.9 8.8 %all_gather.17 = bf16[4,1,512]{2,1,0:T(2,128)(2,1)S(1)} all-gather(bf16[1,1,512]{2,1,0:T(2,128)(2,1)S(1)} %fusion.54), channel_id=1, replica_groups=mesh['tri_0'=4,'tri_1'=16,'sub'=8] {'tri_0'}, dimensions={0}, use_global_device_ids=true | all-gather | bytes 5120 | tf_op jit(solution)/shard_map/all_gather | solution.py:22
  69.7 23.8 %all_gather.18 = bf16[64,1,512]{2,1,0:T(2,128)(2,1)S(1)} all-gather(bf16[4,1,512]{2,1,0:T(2,128)(2,1)S(1)} %all_gather.17), channel_id=1, replica_groups=mesh['tri_0'=4,'tri_1'=16,'sub'=8] {'tri_1'}, dimensions={0}, use_global_device_ids=true | all-gather | bytes 69632 | tf_op jit(solution)/shard_map/all_gather | solution.py:22
  93.9 24.0 %all_gather.19 = bf16[512,512]{1,0:T(8,128)(2,1)S(1)} all-gather(bf16[64,512]{1,0:T(8,128)(2,1)S(1)} %bitcast.124), channel_id=1, replica_groups=mesh['tri_0'=4,'tri_1'=16,'sub'=8] {'sub'}, dimensions={0}, use_global_device_ids=true | all-gather | bytes 589824 | tf_op jit(solution)/shard_map/all_gather | solution.py:111
  117.8 0.5 fusion.67
  118.7 1.2 fusion.8
  119.9 0.8 cholesky.266
  120.7 11.7 %cholesky.104 = f32[128,128]{1,0:T(8,128)S(1)} custom-call(f32[128,128]{1,0:T(8,128)S(1)} %cholesky.266), custom_call_target="Cholesky" | custom-call | tf_op jit(solution)/shard_map/jit(cholesky)/cholesky | solution.py:118
  132.4 9.8 %custom-call.34 = f32[1,128,128]{1,2,0:T(8,128)S(1)} custom-call(f32[1,128,128]{2,1,0:T(8,128)S(1)} %get-tuple-element.32), custom_call_target="InvertDiagBlocksLowerTriangular" | custom-call | tf_op jit(solution)/shard_map/jit(cholesky)/cholesky | solution.py:118
  142.4 1.2 constant_dynamic-update-slice_fusion
  143.6 1.3 convolution_subtract_fusion.6
  144.9 11.7 %cholesky.217 = f32[128,128]{1,0:T(8,128)S(1)} custom-call(f32[128,128]{1,0:T(8,128)S(1)} %cholesky.270), custom_call_target="Cholesky" | custom-call | tf_op jit(solution)/shard_map/jit(cholesky)/cholesky | solution.py:118
  156.7 10.0 %custom-call.35 = f32[1,128,128]{1,2,0:T(8,128)S(1)} custom-call(f32[1,128,128]{2,1,0:T(8,128)S(1)} %get-tuple-element.29), custom_call_target="InvertDiagBlocksLowerTriangular" | custom-call | tf_op jit(solution)/shard_map/jit(cholesky)/cholesky | solution.py:118
  166.9 1.3 convolution_subtract_fusion.7
  168.2 11.7 %cholesky.238 = f32[128,128]{1,0:T(8,128)S(1)} custom-call(f32[128,128]{1,0:T(8,128)S(1)} %cholesky.275), custom_call_target="Cholesky" | custom-call | tf_op jit(solution)/shard_map/jit(cholesky)/cholesky | solution.py:118
  179.9 9.8 %custom-call.36 = f32[1,128,128]{1,2,0:T(8,128)S(1)} custom-call(f32[1,128,128]{2,1,0:T(8,128)S(1)} %get-tuple-element.26), custom_call_target="InvertDiagBlocksLowerTriangular" | custom-call | tf_op jit(solution)/shard_map/jit(cholesky)/cholesky | solution.py:118
  190.4 0.6 gather_fusion.3
  191.0 10.1 %all-gather = bf16[32,2048]{1,0:T(8,128)(2,1)} all-gather(bf16[8,2048]{1,0:T(8,128)(2,1)S(1)} %gather_fusion.3), channel_id=2, replica_groups=mesh['tri_0'=4,'tri_1'=16,'sub'=8] {'tri_0'}, dimensions={0}, use_global_device_ids=true | all-gather | bytes 163840 | tf_op jit(solution)/shard_map/all_gather | solution.py:22
  201.1 1.2 convolution_subtract_fusion.8
  202.5 11.7 %cholesky.255 = f32[128,128]{1,0:T(8,128)S(1)} custom-call(f32[128,128]{1,0:T(8,128)S(1)} %convolution_subtract_fusion.8), custom_call_target="Cholesky" | custom-call | tf_op jit(solution)/shard_map/jit(cholesky)/cholesky | solution.py:118
  214.2 0.7 compare_reduce_fusion.2
  216.3 0.6 compare_reduce_fusion.1
  217.6 0.6 compare_reduce_fusion
  219.0 10.9 %while.1 = (s32[]{:T(128)}, f32[512,512]{1,0:T(8,128)S(1)}, s32[4,2]{0,1:T(2,128)S(1)}, f32[4,128,128]{2,1,0:T(8,128)}, s32[]{:T(128)}) while((s32[]{:T(128)}, f32[512,512]{1,0:T(8,128)S(1)}, s32[4,2]{0,1:T(2,128)S(1)}, f32[4,128,128]{2,1,0:T(8,128)}, s32[]{:T(128)}) %tuple.27), condition=%wide.while_cond, body=%wide.while_body.sunk | while | flops 2 | bytes 132205 | solution.py:119
  219.1 0.6 fusion.83
  219.7 2.0 bitcast_dynamic-update-slice_fusion.2
  221.8 0.6 fusion.83
  222.4 2.0 bitcast_dynamic-update-slice_fusion.2
  224.6 0.6 fusion.83
  225.2 2.0 bitcast_dynamic-update-slice_fusion.2
  227.3 0.6 fusion.83
  227.9 2.0 bitcast_dynamic-update-slice_fusion.2
  229.9 40.1 %custom-call.37 = f32[4,128,128]{1,2,0:T(8,128)S(1)} custom-call(f32[4,128,128]{2,1,0:T(8,128)} %get-tuple-element.12), custom_call_target="InvertDiagBlocksLowerTriangular" | custom-call | tf_op jit(solution)/shard_map/jit(_cho_solve)/triangular_solve | solution.py:119
  272.2 0.7 copy-done.3
  272.9 1.3 convolution_subtract_fusion.5
  274.3 1.7 copy.28
  276.0 1.2 copy.29
  277.2 2.6 reshape_reshape.6
  279.8 1.0 dynamic-slice_bitcast_fusion
  280.7 1.5 stack.3
  282.3 7.7 %all-to-all-start.2 = ((bf16[8,4,64,512]{3,2,1,0:T(8,128)(2,1)}), bf16[8,4,64,512]{3,2,1,0:T(8,128)(2,1)}, u32[]{:S(2)}, u32[]{:S(2)}) async-start(bf16[8,4,64,512]{3,2,1,0:T(8,128)(2,1)} %stack.3), calls=%async_computation.2 | async-start | bytes 4194304 | tf_op jit(solution)/shard_map/all_to_all | solution.py:115
  291.7 0.5 convolution_subtract_fusion
  292.5 0.7 convolution_subtract_fusion.4
  293.5 1.6 convolution_convert_fusion
  295.2 1.5 gather_fusion.4
  296.6 19.7 %all-to-all-done.2 = bf16[8,4,64,512]{3,2,1,0:T(8,128)(2,1)} async-done(((bf16[8,4,64,512]{3,2,1,0:T(8,128)(2,1)}), bf16[8,4,64,512]{3,2,1,0:T(8,128)(2,1)}, u32[]{:S(2)}, u32[]{:S(2)}) %all-to-all-start.2) | async-done | bytes 2097184 | tf_op jit(solution)/shard_map/all_to_all | solution.py:115
  316.4 1.8 copy.34
  318.2 3.9 %gather_fusion.5 = bf16[10,512,512]{2,1,0:T(8,128)(2,1)} fusion(bf16[4,512,512]{2,1,0:T(8,128)(2,1)S(1)} %bitcast.116, s32[1024]{0:T(1024)S(1)} %pad_clamp_fusion), kind=kCustom, calls=%fused_computation.5 | custom fusion | bytes 10485800 | tf_op jit(solution)/shard_map/gather | solution.py:124
  322.0 5.4 %fusion.1 = f32[1,10,64,512]{3,2,1,0:T(8,128)} fusion(bf16[10,64,512]{2,1,0:T(8,128)(2,1)} %gather_fusion.4, bf16[10,512,512]{2,1,0:T(8,128)(2,1)} %gather_fusion.5, pred[10]{0:T(512)(128)(4,1)S(1)} %and_bitcast_fusion, f32[1,10,64,512]{3,2,1,0:T(8,128)S(1)} %copy-done.2), kind=kOutput, calls=%fused_computation.10 | convolution fusion | flops 336199680 | bytes 8519690 | tf_op jit(solution)/shard_map/qrk,qck->qrc/dot_general | solution.py:125
  (70 shorter events, 7.4 us)
Async XLA Ops:
  6.5 35.5 %copy-start.8 = (f32[4]{0:T(128)S(1)}, f32[4]{0:T(128)}, u32[]{:S(2)}) copy-start(f32[4]{0:T(128)} %constant.245) | copy-start | bytes 52
  11.3 34.9 %all-to-all-start.1 = ((bf16[64,2,256]{2,1,0:T(2,128)(2,1)}), bf16[64,2,256]{2,1,0:T(2,128)(2,1)S(1)}, u32[]{:S(2)}, u32[]{:S(2)}) async-start(bf16[64,2,256]{2,1,0:T(2,128)(2,1)} %reshape.313), calls=%async_computation.1 | async-start | bytes 131072 | tf_op jit(solution)/shard_map/all_to_all | solution.py:99
  46.2 143.8 %all-to-all-start = ((bf16[64,2,1024]{2,1,0:T(2,128)(2,1)}), bf16[64,2,1024]{2,1,0:T(2,128)(2,1)S(1)}, u32[]{:S(2)}, u32[]{:S(2)}) async-start(bf16[64,2,1024]{2,1,0:T(2,128)(2,1)} %reshape.315), calls=%async_computation | async-start | bytes 524288 | tf_op jit(solution)/shard_map/all_to_all | solution.py:96
  60.7 213.5 %all-gather.3.cloned.1.call-start = ((), (), s32[]{:S(2)}) async-start(), calls=%async_computation.3 | async-start | bytes 2228224 | tf_op jit(solution)/shard_map/all_gather | solution.py:22
  270.1 1.7 copy-start.5
  271.3 0.9 copy-start
  272.2 0.7 copy-start.3
  282.3 7.7 %copy-start.6 = (f32[4,128,128]{1,2,0:T(8,128)S(1)}, f32[4,128,128]{1,2,0:T(8,128)}, u32[]{:S(2)}) copy-start(f32[4,128,128]{1,2,0:T(8,128)} %copy-done.5) | copy-start | bytes 786436
  282.3 7.7 %copy-start.7 = (f32[128,512]{1,0:T(8,128)S(1)}, f32[128,512]{1,0:T(8,128)}, u32[]{:S(2)}) copy-start(f32[128,512]{1,0:T(8,128)} %convolution_subtract_fusion.5) | copy-start | bytes 786436
  282.3 8.5 %copy-start.4 = (f32[128,512]{1,0:T(8,128)S(1)}, f32[128,512]{1,0:T(8,128)}, u32[]{:S(2)}) copy-start(f32[128,512]{1,0:T(8,128)} %copy-done.3) | copy-start | bytes 786436
  282.3 34.1 %all-to-all-start.2 = ((bf16[8,4,64,512]{3,2,1,0:T(8,128)(2,1)}), bf16[8,4,64,512]{3,2,1,0:T(8,128)(2,1)}, u32[]{:S(2)}, u32[]{:S(2)}) async-start(bf16[8,4,64,512]{3,2,1,0:T(8,128)(2,1)} %stack.3), calls=%async_computation.2 | async-start | bytes 4194304 | tf_op jit(solution)/shard_map/all_to_all | solution.py:115
  290.0 1.6 copy-start.1
  318.1 3.9 %copy-start.2 = (f32[1,10,64,512]{3,2,1,0:T(8,128)S(1)}, f32[1,10,64,512]{3,2,1,0:T(8,128)}, u32[]{:S(2)}) copy-start(f32[1,10,64,512]{3,2,1,0:T(8,128)} %param.9) | copy-start | bytes 3932164
Sparse Core Ops, SparseCore 0:
  201.2 63.6 all-gather.2
